TPU v7x, 32 devices: a whole 2x2x4 slice. The times are simulated.
32 devices in a mesh: dp: 4 (over z), wide: 8 (over y, x, core).
Axes of the slice: x: 2, y: 2, z: 4, core: 2. Of those that a mesh axis runs over, the one named last changes fastest.
Arguments:
- row_ids: int32 [32768, 2, 26], P(('dp', 'wide')), may hold values from 0 to 8191, as said below
- dense_in: float32 [32768, 13], P(('dp', 'wide')), may hold values from -16 to 16
- tables: bfloat16 [26, 262144, 16], P(None, ('dp', 'wide')), may hold values from -6 to 6
- cotangent: bfloat16 [32768, 768], P(('dp', 'wide')), may hold values from -8 to 8
- in_weight: float32 [6, 512, 256], P(None, 'wide'), may hold values from -0.25 to 0.25
- in_momentum: float32 [6, 512, 256], P(None, 'wide'), may hold values from -112 to 112
- in_average: float32 [6, 512, 256], P(None, 'wide'), may hold values from -0.25 to 0.25
- mid_weight: float32 [6, 256, 256], P(None, 'wide'), may hold values from -0.375 to 0.375
- mid_momentum: float32 [6, 256, 256], P(None, 'wide'), may hold values from -160 to 160
- mid_average: float32 [6, 256, 256], P(None, 'wide'), may hold values from -0.375 to 0.375
- norm_weight: float32 [6, 2, 256], P(None, None, 'wide'), may hold values from -1.5 to 1.5, as said below
- norm_momentum: float32 [6, 2, 256], P(None, None, 'wide'), may hold values from -320 to 320
- norm_average: float32 [6, 2, 256], P(None, None, 'wide'), may hold values from -1.5 to 1.5, as said below
- gate_weight: float32 [512, 14], P('wide'), may hold values from -0.25 to 0.25
- gate_momentum: float32 [512, 14], P('wide'), may hold values from -224 to 224
- gate_average: float32 [512, 14], P('wide'), may hold values from -0.25 to 0.25
- dense_weight: float32 [13, 96], P(None, 'wide'), may hold values from -1.75 to 1.75
- dense_momentum: float32 [13, 96], P(None, 'wide'), may hold values from -320 to 320
- dense_average: float32 [13, 96], P(None, 'wide'), may hold values from -1.75 to 1.75
Outputs:
- gate_outputs: bfloat16 [32768, 768], P(('dp', 'wide'))
- dense_grad: float32 [32768, 13], P(('dp', 'wide'))
- table_grad: float32 [26, 262144, 16], P(None, ('dp', 'wide'))
- new_in_weight: float32 [6, 512, 256], P(None, 'wide')
- new_in_momentum: float32 [6, 512, 256], P(None, 'wide')
- new_in_average: float32 [6, 512, 256], P(None, 'wide')
- new_mid_weight: float32 [6, 256, 256], P(None, 'wide')
- new_mid_momentum: float32 [6, 256, 256], P(None, 'wide')
- new_mid_average: float32 [6, 256, 256], P(None, 'wide')
- new_norm_weight: float32 [6, 2, 256], P(None, None, 'wide')
- new_norm_momentum: float32 [6, 2, 256], P(None, None, 'wide')
- new_norm_average: float32 [6, 2, 256], P(None, None, 'wide')
- new_gate_weight: float32 [512, 14], P('wide')
- new_gate_momentum: float32 [512, 14], P('wide')
- new_gate_average: float32 [512, 14], P('wide')
- new_dense_weight: float32 [13, 96], P(None, 'wide')
- new_dense_momentum: float32 [13, 96], P(None, 'wide')
- new_dense_average: float32 [13, 96], P(None, 'wide')
Inputs may be any that keep to these rules, and one draw needn't show every extreme that they name: row_ids[e, 0, f] is a device index along dp+wide, from 0 to 31, and row_ids[e, 1, f] a row of that device, from 0 to 8191; the o-th device along dp+wide holds rows o * 8192 to (o + 1) * 8192 - 1 of every table. Of the lookups of one device's 1024 events (aligned blocks), at most 1248 fall on the rows of one device; in every draw one device receives exactly 1248 from every device. `norm_weight`: row 0 lies between 0.5 and 1.5. `norm_average`: row 0 lies between 0.5 and 1.5.
All inputs are finite; a program needn't handle non-finite values.
Results may differ from a plain program's by a relative error of at most 0.0097.
Values may be sent and summed in bfloat16 or wider, within the bound.
No kernel may reach another device: no remote copies, remote signals or barrier semaphores. Data moves between devices by JAX's collectives and lax.ppermute only.
A program may use at most 256 MiB of HBM per device.

v0:
```python
import math

import jax
import jax.numpy as jnp
from jax import lax
from jax.sharding import PartitionSpec as P

EPS = 1e-05
MOMENTUM = 0.5
AVERAGE = 0.5
HIGH = lax.Precision.HIGHEST
BLOCK_ROWS = 512


def layer_norm(hidden, gain, shift):
    centre = hidden - jnp.mean(hidden, axis=-1, keepdims=True)
    inv_std = lax.rsqrt(jnp.mean(centre * centre, axis=-1, keepdims=True) + EPS)
    normal = centre * inv_std
    return (normal * gain + shift, normal, inv_std)


def gelu_grad(preact, upstream):
    return jax.vjp(jax.nn.gelu, preact)[1](upstream)[0]


def softmax_back(probs, upstream):
    return probs * (upstream - jnp.sum(probs * upstream, axis=-1, keepdims=True))


def update(weight, momentum, average, grad, rate):
    new_momentum = MOMENTUM * momentum + grad
    new_weight = weight - rate * (grad + MOMENTUM * new_momentum)
    new_average = AVERAGE * average + (1.0 - AVERAGE) * new_weight
    return (new_weight, new_momentum, new_average)


def packing_for(columns, count):
    return math.gcd(128 // columns, count)


def lane_pick(wide_rows, lane_of, packing, columns):
    split_rows = wide_rows.reshape(wide_rows.shape[:-1] + (packing, columns)).astype(jnp.float32)
    chosen = lane_of[..., None] == jnp.arange(packing, dtype=jnp.int32)
    return jnp.sum(jnp.where(chosen[..., None], split_rows, 0.0), axis=-2)


def lane_spread(values, lane_of, packing):
    chosen = lane_of[..., None] == jnp.arange(packing, dtype=jnp.int32)
    spread = jnp.where(chosen[..., None], values[..., None, :], 0.0)
    return spread.reshape(values.shape[:-1] + (packing * values.shape[-1],))


def owner_positions(owners, devices):
    lookups = owners.shape[0]
    blocks = -(-lookups // BLOCK_ROWS)
    padding = jnp.full((blocks * BLOCK_ROWS - lookups,), devices, jnp.int32)
    padded = jnp.concatenate([owners, padding]).reshape(blocks, BLOCK_ROWS)
    onehot = (padded[..., None] == jnp.arange(devices, dtype=jnp.int32)).astype(jnp.bfloat16)
    steps = jnp.arange(BLOCK_ROWS, dtype=jnp.int32)
    lower = (steps[:, None] > steps[None, :]).astype(jnp.bfloat16)
    before = jnp.einsum("ij,bjd->bid", lower, onehot, preferred_element_type=jnp.float32)
    totals = jnp.sum(onehot.astype(jnp.float32), axis=1)
    offsets = jnp.cumsum(totals, axis=0) - totals
    counted = jnp.sum((before + offsets[:, None, :]) * onehot.astype(jnp.float32), axis=-1)
    return counted.reshape(-1).astype(jnp.int32)


def local(
    row_ids,
    dense_in,
    tables,
    cotangent,
    in_weight,
    in_momentum,
    in_average,
    mid_weight,
    mid_momentum,
    mid_average,
    norm_weight,
    norm_momentum,
    norm_average,
    gate_weight,
    gate_momentum,
    gate_average,
    dense_weight,
    dense_momentum,
    dense_average,
):
    events = row_ids.shape[0]
    fields = row_ids.shape[2]
    rows_dev = tables.shape[1]
    columns = tables.shape[2]
    devices = lax.axis_size(("dp", "wide"))
    total_events = events * devices
    lookups = events * fields
    capacity = 3 * lookups // (2 * devices)
    in_b, mid_b, norm_b, gate_b, dense_b = (
        lax.all_gather(in_weight.astype(jnp.bfloat16), "wide", axis=1, tiled=True),
        lax.all_gather(mid_weight.astype(jnp.bfloat16), "wide", axis=1, tiled=True),
        lax.all_gather(norm_weight.astype(jnp.bfloat16), "wide", axis=2, tiled=True),
        lax.all_gather(gate_weight.astype(jnp.bfloat16), "wide", axis=0, tiled=True),
        lax.all_gather(dense_weight.astype(jnp.bfloat16), "wide", axis=1, tiled=True),
    )
    sums = lax.psum(
        (jnp.sum(dense_in, axis=0), jnp.sum(dense_in * dense_in, axis=0)), ("dp", "wide")
    )
    mean_dense = sums[0] / total_events
    variance = sums[1] / total_events - mean_dense * mean_dense
    inv_dense = lax.rsqrt(variance + EPS)
    normed = (dense_in - mean_dense) * inv_dense
    dense_full = dense_b.astype(jnp.float32)
    projected = jnp.dot(normed, dense_full, precision=HIGH)
    owners = row_ids[:, 0, :].reshape(lookups)
    local_rows = row_ids[:, 1, :].reshape(lookups)
    field_of = jnp.arange(lookups, dtype=jnp.int32) % fields
    codes = field_of * rows_dev + local_rows
    slots = owners * capacity + owner_positions(owners, devices)
    request = (
        jnp.full((devices * capacity,), -1, jnp.int32)
        .at[slots]
        .set(codes)
        .reshape(devices, capacity)
    )
    table_count = fields * rows_dev
    table_pack = packing_for(columns, table_count)
    wide_table = tables.reshape(table_count // table_pack, table_pack * columns)
    slot_count = devices * capacity
    slot_pack = packing_for(columns, slot_count)
    wanted = lax.all_to_all(request, ("dp", "wide"), split_axis=0, concat_axis=0, tiled=True)
    valid = wanted >= 0
    safe_keys = jnp.where(valid, wanted, 0)
    picked = lane_pick(
        wide_table[safe_keys // table_pack], safe_keys % table_pack, table_pack, columns
    )
    fetched_rows = jnp.where(valid[..., None], picked, 0.0).astype(jnp.bfloat16)
    returned = lax.all_to_all(fetched_rows, ("dp", "wide"), split_axis=0, concat_axis=0, tiled=True)
    wide_fetched = returned.reshape(slot_count // slot_pack, slot_pack * columns)
    looked = lane_pick(wide_fetched[slots // slot_pack], slots % slot_pack, slot_pack, columns)
    looked = looked.astype(jnp.bfloat16).reshape(events, fields * columns)
    features = jnp.concatenate([looked, projected.astype(jnp.bfloat16)], axis=1)
    logits = jnp.dot(features, gate_b, preferred_element_type=jnp.float32)
    gate_a = jax.nn.softmax(logits[:, 0:4], axis=-1)
    gate_bb = jax.nn.softmax(logits[:, 4:8], axis=-1)
    gate_s = jax.nn.softmax(logits[:, 8:14], axis=-1)
    blank = jnp.zeros_like(gate_a[:, 0:2])
    row_a = jnp.concatenate([gate_a[:, 0:2], blank, gate_a[:, 2:4]], axis=1)
    row_b = jnp.concatenate([blank, gate_bb], axis=1)
    mixing = jnp.stack([row_a, row_b, gate_s], axis=1)
    pre_in = jnp.einsum("bd,edh->ebh", features, in_b, preferred_element_type=jnp.float32)
    hidden_in = jax.nn.gelu(pre_in).astype(jnp.bfloat16)
    pre_mid = jnp.einsum("ebh,ehk->ebk", hidden_in, mid_b, preferred_element_type=jnp.float32)
    hidden_mid = jax.nn.gelu(pre_mid)
    norm_full = norm_b.astype(jnp.float32)
    gain = norm_full[:, 0:1, :]
    expert_out, normal, inv_std = layer_norm(hidden_mid, gain, norm_full[:, 1:2, :])
    mixed = jnp.einsum("bge,ebh->bgh", mixing, expert_out, precision=HIGH)
    gate_outputs = mixed.reshape(events, -1).astype(jnp.bfloat16)
    upstream = cotangent.astype(jnp.float32).reshape(events, 3, -1)
    d_out = jnp.einsum("bge,bgh->ebh", mixing, upstream, precision=HIGH)
    d_mixing = jnp.einsum("bgh,ebh->bge", upstream, expert_out, precision=HIGH)
    grad_a = softmax_back(
        gate_a, jnp.concatenate([d_mixing[:, 0, 0:2], d_mixing[:, 0, 4:6]], axis=1)
    )
    grad_b = softmax_back(gate_bb, d_mixing[:, 1, 2:6])
    grad_s = softmax_back(gate_s, d_mixing[:, 2, :])
    d_logits = jnp.concatenate([grad_a, grad_b, grad_s], axis=1).astype(jnp.bfloat16)
    norm_grad = jnp.stack([jnp.sum(d_out * normal, axis=1), jnp.sum(d_out, axis=1)], axis=1)
    d_norm = d_out * gain
    d_mid = inv_std * (
        d_norm
        - jnp.mean(d_norm, axis=-1, keepdims=True)
        - normal * jnp.mean(d_norm * normal, axis=-1, keepdims=True)
    )
    d_pre_mid = gelu_grad(pre_mid, d_mid).astype(jnp.bfloat16)
    mid_grad = jnp.einsum("ebh,ebk->ehk", hidden_in, d_pre_mid, preferred_element_type=jnp.float32)
    d_hidden = jnp.einsum("ebk,ehk->ebh", d_pre_mid, mid_b, preferred_element_type=jnp.float32)
    d_pre_in = gelu_grad(pre_in, d_hidden).astype(jnp.bfloat16)
    in_grad = jnp.einsum("bd,ebh->edh", features, d_pre_in, preferred_element_type=jnp.float32)
    gate_grad = jnp.einsum("bd,bk->dk", features, d_logits, preferred_element_type=jnp.float32)
    d_features = jnp.einsum("ebh,edh->bd", d_pre_in, in_b, preferred_element_type=jnp.float32)
    d_features = d_features + jnp.einsum(
        "bk,dk->bd", d_logits, gate_b, preferred_element_type=jnp.float32
    )
    d_looked = d_features[:, : fields * columns]
    d_projected = d_features[:, fields * columns :]
    dense_grad_w = jnp.einsum("bi,bo->io", normed, d_projected, precision=HIGH)
    d_normed = jnp.einsum("bo,io->bi", d_projected, dense_full, precision=HIGH)
    spread_out = lane_spread(d_looked.reshape(lookups, columns), slots % slot_pack, slot_pack)
    outgoing = (
        jnp.zeros((slot_count // slot_pack, slot_pack * columns), jnp.float32)
        .at[slots // slot_pack]
        .add(spread_out)
    )
    arrived = lax.all_to_all(
        outgoing.reshape(devices, capacity, columns),
        ("dp", "wide"),
        split_axis=0,
        concat_axis=0,
        tiled=True,
    )
    valid_in = wanted >= 0
    target_keys = jnp.where(valid_in, wanted, 0).reshape(-1)
    target_rows = jnp.where(valid_in, wanted // table_pack, table_count // table_pack).reshape(-1)
    spread_in = lane_spread(arrived.reshape(-1, columns), target_keys % table_pack, table_pack)
    table_grad = jax.ops.segment_sum(
        spread_in, target_rows, num_segments=table_count // table_pack + 1
    )
    table_grad = table_grad[: table_count // table_pack].reshape(fields, rows_dev, columns)
    back_sum = jnp.sum(d_normed, axis=0)
    back_cross = jnp.sum(d_normed * normed, axis=0)
    shards = (
        lax.psum_scatter(in_grad, "wide", scatter_dimension=1, tiled=True),
        lax.psum_scatter(mid_grad, "wide", scatter_dimension=1, tiled=True),
        lax.psum_scatter(norm_grad, "wide", scatter_dimension=2, tiled=True),
        lax.psum_scatter(gate_grad, "wide", scatter_dimension=0, tiled=True),
        lax.psum_scatter(dense_grad_w, "wide", scatter_dimension=1, tiled=True),
    )
    grads = lax.psum((shards[0], shards[1], shards[2], shards[3], shards[4]), "dp")
    total_sum, total_cross = lax.psum((back_sum, back_cross), ("dp", "wide"))
    dense_grad = inv_dense * (
        d_normed - total_sum / total_events - normed * total_cross / total_events
    )
    scale = 1.0 / math.sqrt(total_events)
    new_in = update(in_weight, in_momentum, in_average, grads[0], 0.3 * scale)
    new_mid = update(mid_weight, mid_momentum, mid_average, grads[1], 0.3 * scale)
    new_norm = update(norm_weight, norm_momentum, norm_average, grads[2], 0.6 * scale)
    new_gate = update(gate_weight, gate_momentum, gate_average, grads[3], 0.15 * scale)
    new_dense = update(dense_weight, dense_momentum, dense_average, grads[4], 0.6 * scale)
    return (
        gate_outputs,
        dense_grad,
        table_grad,
        new_in[0],
        new_in[1],
        new_in[2],
        new_mid[0],
        new_mid[1],
        new_mid[2],
        new_norm[0],
        new_norm[1],
        new_norm[2],
        new_gate[0],
        new_gate[1],
        new_gate[2],
        new_dense[0],
        new_dense[1],
        new_dense[2],
    )


def solution(mesh):
    return jax.shard_map(
        local,
        mesh=mesh,
        in_specs=(
            P(("dp", "wide"), None, None),
            P(("dp", "wide"), None),
            P(None, ("dp", "wide"), None),
            P(("dp", "wide"), None),
            P(None, "wide", None),
            P(None, "wide", None),
            P(None, "wide", None),
            P(None, "wide", None),
            P(None, "wide", None),
            P(None, "wide", None),
            P(None, None, "wide"),
            P(None, None, "wide"),
            P(None, None, "wide"),
            P("wide", None),
            P("wide", None),
            P("wide", None),
            P(None, "wide"),
            P(None, "wide"),
            P(None, "wide"),
        ),
        out_specs=(
            P(("dp", "wide"), None),
            P(("dp", "wide"), None),
            P(None, ("dp", "wide"), None),
            P(None, "wide", None),
            P(None, "wide", None),
            P(None, "wide", None),
            P(None, "wide", None),
            P(None, "wide", None),
            P(None, "wide", None),
            P(None, None, "wide"),
            P(None, None, "wide"),
            P(None, None, "wide"),
            P("wide", None),
            P("wide", None),
            P("wide", None),
            P(None, "wide"),
            P(None, "wide"),
            P(None, "wide"),
        ),
        check_vma=False,
    )
```

profile of v0, /device:TPU:1, one launch (start us, length us, event | category | flops | bytes accessed | tf_op | source)
XLA Modules:
  0.0 1520.7 jit_solution(13673190681117074929)
XLA Ops:
  15.2 97.7 %scatter_custom_fusion = s32[39936]{0:T(1024)S(1)} fusion(s32[26624]{0:T(1024)S(1)} %bitcast.167, s32[26624]{0:T(1024)S(1)} %fusion.50, s32[]{:T(128)} %constant.120.clone.1), kind=kCustom, calls=%fused_computation.126 | custom fusion | bytes 159748 | tf_op jit(solution)/shard_map/scatter | solution.py:121
  132.0 38.0 %all-reduce.3 = (f32[13]{0:T(128)S(1)}, f32[13]{0:T(128)S(1)}) all-reduce(f32[13]{0:T(128)S(1)} %get-tuple-element.137, f32[13]{0:T(128)S(1)} %get-tuple-element.136), channel_id=1, replica_groups=mesh['dp'=4,'wide'=8] {'dp','wide'}, use_global_device_ids=true, to_apply=%region_9.10 | all-reduce | flops 26 | bytes 208 | tf_op jit(solution)/shard_map/psum | solution.py:104
  170.4 13.7 all_gather.18
  207.4 38.4 %copy.267 = bf16[26,8192,16]{2,1,0:T(8,128)(2,1)} copy(bf16[26,8192,16]{1,2,0:T(8,128)(2,1)} %param.21) | data formatting | bytes 13631488 | tf_op args[2]
  245.8 58.4 %reshape.473 = bf16[26624,128]{1,0:T(8,128)(2,1)} reshape(bf16[26,8192,16]{2,1,0:T(8,128)(2,1)} %copy.267) | data formatting | bytes 13631488 | tf_op jit(solution)/shard_map/reshape | solution.py:126
  308.3 138.0 %gather_fusion = bf16[39936,128]{1,0:T(8,128)(2,1)} fusion(bf16[26624,128]{1,0:T(8,128)(2,1)} %reshape.473, s32[39936]{0:T(1024)S(1)} %broadcast_clamp_fusion), kind=kCustom, calls=%fused_computation | custom fusion | bytes 20606976 | tf_op jit(solution)/shard_map/gather | solution.py:133
  446.3 14.7 copy.268
  461.1 24.1 %reshape.478 = f32[32,1248,8,16]{1,0,3,2:T(8,128)} reshape(f32[39936,128]{0,1:T(8,128)} %copy.268) | data formatting | bytes 40894464 | tf_op jit(solution)/shard_map/convert_element_type | solution.py:42
  502.0 29.0 %all-to-all-done.1 = bf16[32,1248,16]{1,2,0:T(8,128)(2,1)} async-done(((bf16[32,1248,16]{1,2,0:T(8,128)(2,1)}), bf16[32,1248,16]{1,2,0:T(8,128)(2,1)}, u32[]{:S(2)}, u32[]{:S(2)}) %all-to-all-start.1) | async-done | bytes 1277984 | tf_op jit(solution)/shard_map/all_to_all | solution.py:136
  539.0 11.1 reshape.474
  550.1 92.9 %gather_fusion.1 = bf16[26624,128]{1,0:T(8,128)(2,1)} fusion(bf16[4992,128]{1,0:T(8,128)(2,1)S(1)} %reshape.474, s32[26624]{0:T(1024)S(1)} %broadcast_clamp_fusion.1), kind=kCustom, calls=%fused_computation.1 | custom fusion | bytes 13737984 | tf_op jit(solution)/shard_map/gather | solution.py:138
  643.0 10.3 copy.271
  783.2 14.5 copy.297
  797.7 142.3 %scatter_custom_fusion.1 = f32[4992,128]{1,0:T(8,128)S(1)} fusion(s32[26624]{0:T(1024)} %bitcast.164, f32[26624,128]{1,0:T(8,128)} %copy.297, f32[]{:T(128)} %constant.116.clone.1), kind=kCustom, calls=%fused_computation.60 | custom fusion | flops 3407872 | bytes 2556416 | tf_op jit(solution)/shard_map/scatter-add | solution.py:192
  949.8 12.2 copy.298
  969.4 76.7 %all-reduce.2 = (f32[13]{0:T(128)S(1)}, f32[13]{0:T(128)S(1)}) all-reduce(f32[13]{0:T(128)S(1)} %get-tuple-element.131, f32[13]{0:T(128)S(1)} %get-tuple-element.130), channel_id=1, replica_groups=mesh['dp'=4,'wide'=8] {'dp','wide'}, use_global_device_ids=true, to_apply=%region_26.27 | all-reduce | flops 26 | bytes 208 | tf_op jit(solution)/shard_map/psum | solution.py:219
  1046.0 15.6 %fusion.28 = bf16[1024,3,256]{2,1,0:T(4,128)(2,1)} fusion(f32[1024,3,6]{2,1,0:T(4,128)S(1)} %copy-done.3, f32[6,1024,256]{2,1,0:T(8,128)} %copy-done.1), kind=kOutput, calls=%fused_computation.56 | convolution fusion | flops 57409536 | bytes 7938048 | tf_op jit(solution)/shard_map/bge,ebh->bgh/dot_general | solution.py:156
  1067.7 12.9 all-reduce.1
  1083.1 14.0 all-reduce.4
  1106.2 10.9 broadcast_select_fusion
  1117.1 21.2 %copy.300 = f32[39936,128]{1,0:T(8,128)} copy(f32[39936,128]{0,1:T(8,128)} %bitcast.149) | data formatting | bytes 40894464 | tf_op jit(solution)/shard_map/jit(_where)/select_n | solution.py:49
  1138.3 238.8 %scatter_custom_fusion.2 = f32[26625,128]{1,0:T(8,128)} fusion(s32[39936]{0:T(1024)S(1)} %bitcast.165, f32[39936,128]{1,0:T(8,128)} %copy.300, f32[]{:T(128)} %constant.116.clone.1), kind=kCustom, calls=%fused_computation.16 | custom fusion | flops 5111808 | bytes 13632512 | tf_op jit(solution)/shard_map/scatter-add | solution.py:205
  1387.0 60.3 %reshape.477 = f32[26,8192,16]{2,1,0:T(8,128)} reshape(f32[26624,128]{1,0:T(8,128)} %slice.81) | data formatting | bytes 27262976 | tf_op jit(solution)/shard_map/reshape | solution.py:208
  1447.3 60.1 %copy.311 = f32[26,8192,16]{1,2,0:T(8,128)} copy(f32[26,8192,16]{2,1,0:T(8,128)} %reshape.477) | data formatting | bytes 27262976
  (291 shorter events, 258.8 us)
Async XLA Ops:
  7.2 666.8 %all-gather.4.cloned.1.call-start = ((), (), s32[]{:S(2)}) async-start(), calls=%async_computation.7 | async-start | bytes 1769472 | tf_op jit(solution)/shard_map/all_gather | solution.py:98
  10.7 110.7 %copy-start.11 = (f32[1024,13]{0,1:T(8,128)S(1)}, f32[1024,13]{0,1:T(8,128)}, u32[]{:S(2)}) copy-start(f32[1024,13]{0,1:T(8,128)} %param.20) | copy-start | bytes 159748
  10.7 110.8 %copy-start.42 = (f32[64,14]{0,1:T(8,128)S(1)}, f32[64,14]{0,1:T(8,128)}, u32[]{:S(2)}) copy-start(f32[64,14]{0,1:T(8,128)} %param.32) | copy-start | bytes 10756
  10.7 110.8 %copy-start.44 = (f32[13,12]{1,0:T(8,128)S(1)}, f32[13,12]{1,0:T(8,128)}, u32[]{:S(2)}) copy-start(f32[13,12]{1,0:T(8,128)} %param.35) | copy-start | bytes 1876
  10.7 120.4 %copy-start.19 = (f32[6,32,256]{2,1,0:T(8,128)S(1)}, f32[6,32,256]{2,1,0:T(8,128)}, u32[]{:S(2)}) copy-start(f32[6,32,256]{2,1,0:T(8,128)} %param.26) | copy-start | bytes 589828
  12.1 172.0 %copy-start.46 = (f32[6,2,32]{2,1,0:T(2,128)S(1)}, f32[6,2,32]{2,1,0:T(2,128)}, u32[]{:S(2)}) copy-start(f32[6,2,32]{2,1,0:T(2,128)} %param.29) | copy-start | bytes 4612
  12.1 190.7 %copy-start.14 = (bf16[1024,768]{1,0:T(8,128)(2,1)S(1)}, bf16[1024,768]{1,0:T(8,128)(2,1)}, u32[]{:S(2)}) copy-start(bf16[1024,768]{1,0:T(8,128)(2,1)} %param.22) | copy-start | bytes 4718596
  15.2 189.2 %copy-start.22 = (s32[26624,1]{0,1:T(1,128)}, s32[26624,1]{0,1:T(1,128)S(1)}, u32[]{:S(2)}) copy-start(s32[26624,1]{0,1:T(1,128)S(1)} %get-tuple-element.165) | copy-start | bytes 319492
  113.9 192.1 %all-to-all-start = ((s32[32,1,1248]{2,1,0:T(1,128)}), s32[32,1,1248]{2,1,0:T(1,128)S(1)}, u32[]{:S(2)}, u32[]{:S(2)}) async-start(s32[32,1,1248]{2,1,0:T(1,128)} %all_to_all.20), calls=%async_computation | async-start | bytes 327680 | tf_op jit(solution)/shard_map/all_to_all | solution.py:129
  131.1 62.0 %copy-start.25 = (bf16[96,13]{1,0:T(8,128)(2,1)}, bf16[96,13]{1,0:T(8,128)(2,1)S(1)}, u32[]{:S(2)}) copy-start(bf16[96,13]{1,0:T(8,128)(2,1)S(1)} %reshape.530) | copy-start | bytes 7492
  193.2 479.1 %copy-start.37 = (bf16[512,14]{0,1:T(8,128)(2,1)}, bf16[512,14]{0,1:T(8,128)(2,1)S(1)}, u32[]{:S(2)}) copy-start(bf16[512,14]{0,1:T(8,128)(2,1)S(1)} %reshape.526) | copy-start | bytes 43012
  207.4 480.7 %copy-start.2 = (bf16[1024,3,256]{2,1,0:T(4,128)(2,1)}, bf16[1024,3,256]{2,1,0:T(4,128)(2,1)S(1)}, u32[]{:S(2)}) copy-start(bf16[1024,3,256]{2,1,0:T(4,128)(2,1)S(1)} %copy.289) | copy-start | bytes 4718596
  306.0 379.2 %copy-start.31 = (f32[6,256]{1,0:T(8,128)}, f32[6,256]{1,0:T(8,128)S(1)}, u32[]{:S(2)}) copy-start(f32[6,256]{1,0:T(8,128)S(1)} %get-tuple-element.179) | copy-start | bytes 18436
  496.2 34.8 %all-to-all-start.1 = ((bf16[32,1248,16]{1,2,0:T(8,128)(2,1)}), bf16[32,1248,16]{1,2,0:T(8,128)(2,1)}, u32[]{:S(2)}, u32[]{:S(2)}) async-start(bf16[32,1248,16]{1,2,0:T(8,128)(2,1)} %copy.269), calls=%async_computation.1 | async-start | bytes 2621440 | tf_op jit(solution)/shard_map/all_to_all | solution.py:136
  499.8 581.6 %reduce-scatter.14.cloned.1.call-start = ((), (), s32[]{:S(2)}) async-start(), calls=%async_computation.10 | async-start | bytes 147456
  741.9 340.3 %reduce-scatter.16.cloned.1.call-start = ((), (), s32[]{:S(2)}) async-start(), calls=%async_computation.11 | async-start | bytes 294912
  743.4 356.7 %reduce-scatter.12.cloned.1.call-start = ((), (), s32[]{:S(2)}) async-start(), calls=%async_computation.9 | async-start | bytes 1769472 | tf_op jit(solution)/shard_map/reduce_scatter | solution.py:213
  962.0 84.0 %copy-start.3 = (f32[1024,3,6]{2,1,0:T(4,128)S(1)}, f32[1024,3,6]{2,1,0:T(4,128)}, u32[]{:S(2)}) copy-start(f32[1024,3,6]{2,1,0:T(4,128)} %copy.284) | copy-start | bytes 221188
  962.0 138.2 %all-to-all-start.2 = ((f32[32,1248,16]{1,2,0:T(8,128)}), f32[32,1248,16]{1,2,0:T(8,128)}, u32[]{:S(2)}, u32[]{:S(2)}) async-start(f32[32,1248,16]{1,2,0:T(8,128)} %copy.298), calls=%async_computation.2 | async-start | bytes 5242880 | tf_op jit(solution)/shard_map/all_to_all | solution.py:194
  966.5 133.6 %reduce-scatter.10.cloned.1.call-start = ((), (), s32[]{:S(2)}) async-start(), calls=%async_computation.8 | async-start | bytes 4718592 | tf_op jit(solution)/shard_map/reduce_scatter | solution.py:212
  967.1 540.3 %all-reduce.8.cloned.1.call-start = ((), (), s32[]{:S(2)}) async-start(), calls=%async_computation.12 | async-start | bytes 1441792 | tf_op jit(solution)/shard_map/psum | solution.py:218
  1447.2 64.6 %copy-start.20 = (f32[6,32,256]{2,1,0:T(8,128)S(1)}, f32[6,32,256]{2,1,0:T(8,128)}, u32[]{:S(2)}) copy-start(f32[6,32,256]{2,1,0:T(8,128)} %param.26) | copy-start | bytes 589828
  1447.2 64.6 %copy-start.27 = (f32[6,32,256]{2,1,0:T(8,128)S(1)}, f32[6,32,256]{2,1,0:T(8,128)}, u32[]{:S(2)}) copy-start(f32[6,32,256]{2,1,0:T(8,128)} %param.28) | copy-start | bytes 589828
  1447.3 64.6 %copy-start.28 = (f32[6,32,256]{2,1,0:T(8,128)S(1)}, f32[6,32,256]{2,1,0:T(8,128)}, u32[]{:S(2)}) copy-start(f32[6,32,256]{2,1,0:T(8,128)} %param.27) | copy-start | bytes 589828
  (52 other events, 912.4 us)
Sparse Core Ops, SparseCore 0:
  10.5 28.1 all-gather.3
  742.1 32.3 reduce-scatter.13
  778.3 33.5 reduce-scatter.15
  815.1 38.9 reduce-scatter.11
  970.4 60.8 reduce-scatter.9
  1100.3 43.6 all-reduce.7
where the time goes:
time: 1540 us; the launch traced here: 1520 us
  local copies, waits for them, and re-layouts  760 us (49%)
  other arithmetic  449 us (29%)
  blocking collectives  182 us (12%)
  matrix products  67.8 us (4%)
  waiting for transfers between devices  29.7 us (2%)
  between operations  16.2 us (1%)
  starting transfers between devices  15.8 us (1%)
    scatter-add x1, other arithmetic, local(): jax.ops.segment_sum(spread_in, target_rows, num_segments=table_count // t...  239 us
    scatter-add x1, other arithmetic, local(): outgoing = jnp.zeros((slot_count // slot_pack, slot_pack * columns), jnp....  142 us
    gather x1, local copies, waits for them, and re-layouts, local(): wide_table[safe_keys // table_pack]  138 us
    unnamed x155, local copies, waits for them, and re-layouts  116 us
    scatter x1, local copies, waits for them, and re-layouts, local(): request = jnp.full((devices * capacity,), -1, jnp.int32).at[slots].set(co...  97.7 us
    gather x1, local copies, waits for them, and re-layouts, local(): wide_fetched[slots // slot_pack]  92.9 us
    psum x1, blocking collectives, local(): total_sum, total_cross = lax.psum((back_sum, back_cross), ('dp', 'wide'))  76.7 us
    reshape x1, local copies, waits for them, and re-layouts, local(): table_grad[:table_count // table_pack].reshape(fields, rows_dev, columns)  60.3 us
  transfers between devices with their start and end apart: 9, of which 1 were waited for; matrix products, arithmetic and copies ran while one was open for 79% of the time, Pallas kernels for 0%

commit v1 on v0

--- a/solution.py
+++ b/solution.py
@@ -1,15 +1,20 @@
+import functools
 import math
 
 import jax
 import jax.numpy as jnp
 from jax import lax
+from jax.experimental import pallas as pl
+from jax.experimental.pallas import tpu as pltpu
 from jax.sharding import PartitionSpec as P
 
 EPS = 1e-05
 MOMENTUM = 0.5
 AVERAGE = 0.5
 HIGH = lax.Precision.HIGHEST
-BLOCK_ROWS = 512
+LANES = 128
+ROW_SPLIT = 512
+VMEM_BYTES = 48 * 1024 * 1024
 
 
 def layer_norm(hidden, gain, shift):
@@ -34,35 +39,418 @@
     return (new_weight, new_momentum, new_average)
 
 
-def packing_for(columns, count):
-    return math.gcd(128 // columns, count)
-
-
-def lane_pick(wide_rows, lane_of, packing, columns):
-    split_rows = wide_rows.reshape(wide_rows.shape[:-1] + (packing, columns)).astype(jnp.float32)
-    chosen = lane_of[..., None] == jnp.arange(packing, dtype=jnp.int32)
-    return jnp.sum(jnp.where(chosen[..., None], split_rows, 0.0), axis=-2)
-
-
-def lane_spread(values, lane_of, packing):
-    chosen = lane_of[..., None] == jnp.arange(packing, dtype=jnp.int32)
-    spread = jnp.where(chosen[..., None], values[..., None, :], 0.0)
-    return spread.reshape(values.shape[:-1] + (packing * values.shape[-1],))
-
-
-def owner_positions(owners, devices):
-    lookups = owners.shape[0]
-    blocks = -(-lookups // BLOCK_ROWS)
-    padding = jnp.full((blocks * BLOCK_ROWS - lookups,), devices, jnp.int32)
-    padded = jnp.concatenate([owners, padding]).reshape(blocks, BLOCK_ROWS)
-    onehot = (padded[..., None] == jnp.arange(devices, dtype=jnp.int32)).astype(jnp.bfloat16)
-    steps = jnp.arange(BLOCK_ROWS, dtype=jnp.int32)
-    lower = (steps[:, None] > steps[None, :]).astype(jnp.bfloat16)
-    before = jnp.einsum("ij,bjd->bid", lower, onehot, preferred_element_type=jnp.float32)
-    totals = jnp.sum(onehot.astype(jnp.float32), axis=1)
-    offsets = jnp.cumsum(totals, axis=0) - totals
-    counted = jnp.sum((before + offsets[:, None, :]) * onehot.astype(jnp.float32), axis=-1)
-    return counted.reshape(-1).astype(jnp.int32)
+def params(**kw):
+    return pltpu.CompilerParams(vmem_limit_bytes=VMEM_BYTES, **kw)
+
+
+def lane_ids(shape, dtype):
+    return lax.broadcasted_iota(dtype, shape, len(shape) - 1)
+
+
+def segment_parts(load, a, d, length, last_tile, lanes):
+    am = a & (LANES - 1)
+    dm = d & (LANES - 1)
+    shift = (dm - am) & (LANES - 1)
+    ta = lax.shift_right_logical(a, 7)
+    r0 = pltpu.roll(load(jnp.minimum(ta, last_tile)), shift, 1)
+    r1 = pltpu.roll(load(jnp.minimum(ta + 1, last_tile)), shift, 1)
+    ahead = dm >= am
+    kind = lanes.dtype
+    cut0 = jnp.where(ahead, LANES, shift).astype(kind)
+    cut1 = jnp.where(ahead, shift, 0).astype(kind)
+    v0 = jnp.where(lanes < cut0, r0, r1)
+    v1 = jnp.where(lanes < cut1, r0, r1)
+    return dm, v0, v1
+
+
+def move_short(load, store, segments, last_tile, last_dst, lanes, first):
+    kind = lanes.dtype
+    cur = first
+    for a, d, length in segments:
+        dm, v0, v1 = segment_parts(load, a, d, length, last_tile, lanes)
+        cur = jnp.where(lanes >= dm.astype(kind), v0, cur)
+        store(jnp.minimum(lax.shift_right_logical(d, 7), last_dst), cur)
+        crossed = jnp.where(dm + length >= LANES, LANES, 0).astype(kind)
+        cur = jnp.where(lanes < crossed, v1, cur)
+    a, d, length = segments[-1]
+    store(jnp.minimum(lax.shift_right_logical(d + length, 7), last_dst), cur)
+
+
+def move_long(load, store, read, segment_at, count, last_tile, last_dst, lanes):
+    kind = lanes.dtype
+
+    def one(i, _):
+        a, d, length = segment_at(i)
+
+        def chunk(k, _):
+            left = jnp.minimum(length - k * LANES, LANES)
+            dk = d + k * LANES
+            dm, v0, v1 = segment_parts(load, a + k * LANES, dk, left, last_tile, lanes)
+            td = lax.shift_right_logical(dk, 7)
+            low = dm.astype(kind)
+            high = (dm + left).astype(kind)
+            keep = (lanes >= low) & (lanes < high)
+            store(td, jnp.where(keep, v0, read(td)))
+            nxt = jnp.minimum(td + 1, last_dst)
+            over = jnp.maximum(dm + left - LANES, 0).astype(kind)
+            store(nxt, jnp.where(lanes < over, v1, read(nxt)))
+            return 0
+
+        lax.fori_loop(0, lax.shift_right_logical(length + LANES - 1, 7), chunk, 0)
+        return 0
+
+    lax.fori_loop(0, count, one, 0)
+
+
+def move(load, store, read, segment_at, count, longest, last_tile, last_dst, lanes, blank):
+    @pl.when(longest <= LANES)
+    def _():
+        if count <= 32:
+            move_short(load, store, [segment_at(i) for i in range(count)], last_tile, last_dst, lanes, blank)
+        else:
+            step = 32
+            assert count % step == 0
+
+            def some(g, _):
+                first = read(jnp.minimum(lax.shift_right_logical(segment_at(g * step)[1], 7), last_dst))
+                move_short(load, store, [segment_at(g * step + i) for i in range(step)], last_tile, last_dst, lanes, first)
+                return 0
+
+            lax.fori_loop(0, count // step, some, 0)
+
+    @pl.when(longest > LANES)
+    def _():
+        move_long(load, store, read, segment_at, count, last_tile, last_dst, lanes)
+
+
+def row_load(ref, base=0):
+    return lambda t: ref[pl.ds(base + t, 1), :]
+
+
+def row_store(ref, base=0):
+    def put(t, v):
+        ref[pl.ds(base + t, 1), :] = v
+    return put
+
+
+def tile_load(ref, base=0):
+    return lambda t: ref[base + t]
+
+
+def tile_store(ref, base=0):
+    def put(t, v):
+        ref[base + t] = v
+    return put
+
+
+def request_kernel(fields, devices, tiles, start_ref, off_ref, cnt_ref, longest_ref, pos_ref, code_ref, counts_ref, out_ref, inv_ref, sorted_ref):
+    f = pl.program_id(0)
+    events = pos_ref.shape[2]
+    ev_tiles = events // LANES
+    code = code_ref[0]
+    event = lane_ids((1, events), jnp.int32)
+    sub = lax.broadcasted_iota(jnp.int32, (16, events), 0)
+    rows = jnp.where(sub == 0, code >> 7, jnp.where(sub == 1, code & 127, jnp.where(sub == 2, event >> 7, jnp.where(sub == 3, event & 127, 0))))
+    rows = rows.astype(jnp.float32).astype(jnp.bfloat16)
+    place = pos_ref[0].astype(jnp.int16)
+    for c in range(events // 256):
+        ids = lax.broadcasted_iota(jnp.int16, (256, events), 0) + jnp.int16(c * 256)
+        onehot = jnp.where(place == ids, jnp.bfloat16(1), jnp.bfloat16(0))
+        got = lax.dot_general(rows, onehot, (((1,), (1,)), ((), ())), preferred_element_type=jnp.float32)
+        got = got.astype(jnp.int32)
+        value = got[0:1] * 128 + got[1:2]
+        inverse = got[2:3] * 128 + got[3:4]
+        inv_ref[0, :, c * 256:(c + 1) * 256] = inverse
+        for h in range(2):
+            sorted_ref[pl.ds(f * ev_tiles + c * 2 + h, 1), :] = value[:, h * 128:(h + 1) * 128]
+
+    @pl.when(f == fields - 1)
+    def _():
+        lanes = lane_ids((1, LANES), jnp.int32)
+        blank = jnp.zeros((1, LANES), jnp.int32)
+
+        def owner(o, _):
+            def segment_at(i):
+                k = i * devices + o
+                return start_ref[k] + i * events, off_ref[k], cnt_ref[k]
+
+            move(row_load(sorted_ref), row_store(out_ref, o * tiles), row_load(out_ref, o * tiles), segment_at, fields, longest_ref[o],
+                 fields * ev_tiles - 1, tiles - 1, lanes, blank)
+            last = o * tiles + tiles - 1
+            tail = out_ref[pl.ds(last, 1), :]
+            out_ref[pl.ds(last, 1), :] = jnp.where(lanes >= LANES - fields, counts_ref[pl.ds(o, 1), :], tail)
+            return 0
+
+        lax.fori_loop(0, devices, owner, 0)
+
+
+def build_request(start, off, cnt, longest, pos, code, counts, tiles):
+    fields, events = pos.shape
+    devices = counts.shape[0]
+    kernel = functools.partial(request_kernel, fields, devices, tiles)
+    return pl.pallas_call(
+        kernel,
+        grid_spec=pltpu.PrefetchScalarGridSpec(
+            num_scalar_prefetch=4,
+            grid=(fields,),
+            in_specs=[
+                pl.BlockSpec((1, 1, events), lambda f, *_: (f, 0, 0)),
+                pl.BlockSpec((1, 1, events), lambda f, *_: (f, 0, 0)),
+                pl.BlockSpec((devices, LANES), lambda f, *_: (0, 0)),
+            ],
+            out_specs=[
+                pl.BlockSpec((devices * tiles, LANES), lambda f, *_: (0, 0)),
+                pl.BlockSpec((1, 1, events), lambda f, *_: (f, 0, 0)),
+            ],
+            scratch_shapes=[pltpu.VMEM((fields * events // LANES, LANES), jnp.int32)],
+        ),
+        out_shape=[
+            jax.ShapeDtypeStruct((devices * tiles, LANES), jnp.int32),
+            jax.ShapeDtypeStruct((fields, 1, events), jnp.int32),
+        ],
+        compiler_params=params(),
+        name="build_request",
+    )(start, off, cnt, longest, pos.reshape(fields, 1, events), code.reshape(fields, 1, events), counts)
+
+
+def fetch_kernel(fields, devices, tiles, soff_ref, fst_ref, cnt_ref, total_ref, base_ref, longf_ref, longs_ref, asked_ref, table_ref, out_ref, codes_ref, vals_ref):
+    f = pl.program_id(0)
+    rows_dev = table_ref.shape[2]
+    parts = rows_dev // ROW_SPLIT
+    slots = devices * tiles
+    fm_tiles = codes_ref.shape[0]
+    base = base_ref[f]
+    lanes = lane_ids((1, LANES), jnp.int32)
+    blank = jnp.zeros((1, LANES), jnp.int32)
+
+    def segment_in(s):
+        k = f * devices + s
+        return soff_ref[k] + s * tiles * LANES, fst_ref[k] + base * LANES, cnt_ref[k]
+
+    move(row_load(asked_ref), row_store(codes_ref), row_load(codes_ref), segment_in, devices, longf_ref[f], slots - 1, fm_tiles - 1, lanes, blank)
+
+    stacked = jnp.concatenate([table_ref[0, :, p * ROW_SPLIT:(p + 1) * ROW_SPLIT] for p in range(parts)], axis=0)
+    ids = lax.broadcasted_iota(jnp.int16, (ROW_SPLIT, 256), 0)
+
+    def pair(t, _):
+        at = base + 2 * t
+        code = jnp.concatenate([codes_ref[pl.ds(at, 1), :], codes_ref[pl.ds(at + 1, 1), :]], axis=1)
+        low = (code & (ROW_SPLIT - 1)).astype(jnp.int16)
+        high = code >> 9
+        onehot = jnp.where(low == ids, jnp.bfloat16(1), jnp.bfloat16(0))
+        wide = jnp.dot(stacked, onehot, preferred_element_type=jnp.float32)
+        got = jnp.zeros((16, 256), jnp.float32)
+        for p in range(parts):
+            got = jnp.where(high == p, wide[p * 16:(p + 1) * 16], got)
+        got = got.astype(jnp.bfloat16)
+        vals_ref[at] = got[:, :LANES]
+        vals_ref[at + 1] = got[:, LANES:]
+        return 0
+
+    lax.fori_loop(0, lax.shift_right_logical(total_ref[f] + 255, 8), pair, 0)
+
+    @pl.when(f == fields - 1)
+    def _():
+        lanes16 = lane_ids((16, LANES), jnp.int16)
+        blank16 = jnp.zeros((16, LANES), jnp.bfloat16)
+
+        def source(s, _):
+            def segment_at(i):
+                k = i * devices + s
+                return fst_ref[k] + base_ref[i] * LANES, soff_ref[k], cnt_ref[k]
+
+            move(tile_load(vals_ref), tile_store(out_ref, s * tiles), tile_load(out_ref, s * tiles), segment_at, fields, longs_ref[s],
+                 fm_tiles - 1, tiles - 1, lanes16, blank16)
+            return 0
+
+        lax.fori_loop(0, devices, source, 0)
+
+
+def fetch_rows(soff, fst, cnt, total, base, longf, longs, asked, tables_t, tiles, fm_tiles):
+    fields, columns, rows_dev = tables_t.shape
+    devices = asked.shape[0] // tiles
+    kernel = functools.partial(fetch_kernel, fields, devices, tiles)
+    return pl.pallas_call(
+        kernel,
+        grid_spec=pltpu.PrefetchScalarGridSpec(
+            num_scalar_prefetch=7,
+            grid=(fields,),
+            in_specs=[
+                pl.BlockSpec((devices * tiles, LANES), lambda f, *_: (0, 0)),
+                pl.BlockSpec((1, columns, rows_dev), lambda f, *_: (f, 0, 0)),
+            ],
+            out_specs=[
+                pl.BlockSpec((devices * tiles, columns, LANES), lambda f, *_: (0, 0, 0)),
+                pl.BlockSpec((fm_tiles, LANES), lambda f, *_: (0, 0)),
+            ],
+            scratch_shapes=[pltpu.VMEM((fm_tiles, columns, LANES), jnp.bfloat16)],
+        ),
+        out_shape=[
+            jax.ShapeDtypeStruct((devices * tiles, columns, LANES), jnp.bfloat16),
+            jax.ShapeDtypeStruct((fm_tiles, LANES), jnp.int32),
+        ],
+        compiler_params=params(),
+        name="fetch_rows",
+    )(soff, fst, cnt, total, base, longf, longs, asked, tables_t)
+
+
+def unsort_kernel(devices, tiles, start_ref, off_ref, cnt_ref, longest_ref, pos_ref, got_ref, out_ref, sorted_ref):
+    f = pl.program_id(0)
+    events = pos_ref.shape[2]
+    ev_tiles = events // LANES
+    lanes16 = lane_ids((16, LANES), jnp.int16)
+    blank16 = jnp.zeros((16, LANES), jnp.bfloat16)
+
+    def segment_at(o):
+        k = f * devices + o
+        return off_ref[k] + o * tiles * LANES, start_ref[k], cnt_ref[k]
+
+    move(tile_load(got_ref), tile_store(sorted_ref), tile_load(sorted_ref), segment_at, devices, longest_ref[f], devices * tiles - 1, ev_tiles, lanes16, blank16)
+    rows = jnp.concatenate([sorted_ref[t] for t in range(ev_tiles)], axis=1)
+    for c in range(events // 256):
+        place = pos_ref[0, :, c * 256:(c + 1) * 256].astype(jnp.int16)
+        ids = lax.broadcasted_iota(jnp.int16, (events, 256), 0)
+        onehot = jnp.where(place == ids, jnp.bfloat16(1), jnp.bfloat16(0))
+        got = jnp.dot(rows, onehot, preferred_element_type=jnp.float32)
+        out_ref[0, :, c * 256:(c + 1) * 256] = got.astype(jnp.bfloat16)
+
+
+def unsort_rows(start, off, cnt, longest, pos, got, tiles):
+    fields, events = pos.shape
+    devices = got.shape[0] // tiles
+    columns = got.shape[1]
+    kernel = functools.partial(unsort_kernel, devices, tiles)
+    return pl.pallas_call(
+        kernel,
+        grid_spec=pltpu.PrefetchScalarGridSpec(
+            num_scalar_prefetch=4,
+            grid=(fields,),
+            in_specs=[
+                pl.BlockSpec((1, 1, events), lambda f, *_: (f, 0, 0)),
+                pl.BlockSpec((devices * tiles, columns, LANES), lambda f, *_: (0, 0, 0)),
+            ],
+            out_specs=pl.BlockSpec((1, columns, events), lambda f, *_: (f, 0, 0)),
+            scratch_shapes=[pltpu.VMEM((events // LANES + 1, columns, LANES), jnp.bfloat16)],
+        ),
+        out_shape=jax.ShapeDtypeStruct((fields, columns, events), jnp.bfloat16),
+        compiler_params=params(),
+        name="unsort_rows",
+    )(start, off, cnt, longest, pos.reshape(fields, 1, events), got)
+
+
+def sort_kernel(fields, devices, tiles, start_ref, off_ref, cnt_ref, longest_ref, inv_ref, grad_ref, out_ref, sorted_ref):
+    f = pl.program_id(0)
+    events = inv_ref.shape[2]
+    ev_tiles = events // LANES
+    rows = grad_ref[0]
+    for c in range(events // 256):
+        place = inv_ref[0, :, c * 256:(c + 1) * 256].astype(jnp.int16)
+        ids = lax.broadcasted_iota(jnp.int16, (events, 256), 0)
+        onehot = jnp.where(place == ids, jnp.bfloat16(1), jnp.bfloat16(0))
+        got = jnp.dot(rows, onehot, preferred_element_type=jnp.float32).astype(jnp.bfloat16)
+        for h in range(2):
+            sorted_ref[f * ev_tiles + c * 2 + h] = got[:, h * 128:(h + 1) * 128]
+
+    @pl.when(f == fields - 1)
+    def _():
+        lanes16 = lane_ids((16, LANES), jnp.int16)
+        blank16 = jnp.zeros((16, LANES), jnp.bfloat16)
+
+        def owner(o, _):
+            def segment_at(i):
+                k = i * devices + o
+                return start_ref[k] + i * events, off_ref[k], cnt_ref[k]
+
+            move(tile_load(sorted_ref), tile_store(out_ref, o * tiles), tile_load(out_ref, o * tiles), segment_at, fields, longest_ref[o],
+                 fields * ev_tiles - 1, tiles - 1, lanes16, blank16)
+            return 0
+
+        lax.fori_loop(0, devices, owner, 0)
+
+
+def sort_grads(start, off, cnt, longest, inv, grads, tiles):
+    fields, columns, events = grads.shape
+    devices = start.shape[0] // fields
+    kernel = functools.partial(sort_kernel, fields, devices, tiles)
+    return pl.pallas_call(
+        kernel,
+        grid_spec=pltpu.PrefetchScalarGridSpec(
+            num_scalar_prefetch=4,
+            grid=(fields,),
+            in_specs=[
+                pl.BlockSpec((1, 1, events), lambda f, *_: (f, 0, 0)),
+                pl.BlockSpec((1, columns, events), lambda f, *_: (f, 0, 0)),
+            ],
+            out_specs=pl.BlockSpec((devices * tiles, columns, LANES), lambda f, *_: (0, 0, 0)),
+            scratch_shapes=[pltpu.VMEM((fields * events // LANES, columns, LANES), jnp.bfloat16)],
+        ),
+        out_shape=jax.ShapeDtypeStruct((devices * tiles, columns, LANES), jnp.bfloat16),
+        compiler_params=params(),
+        name="sort_grads",
+    )(start, off, cnt, longest, inv, grads)
+
+
+def add_kernel(fields, devices, tiles, soff_ref, fst_ref, cnt_ref, total_ref, base_ref, longf_ref, codes_ref, grads_ref, out_ref, vals_ref, sum_ref):
+    f = pl.program_id(0)
+    rows_dev = out_ref.shape[2]
+    parts = rows_dev // ROW_SPLIT
+    slots = devices * tiles
+    base = base_ref[f]
+    total = total_ref[f]
+    lanes16 = lane_ids((16, LANES), jnp.int16)
+    blank16 = jnp.zeros((16, LANES), jnp.bfloat16)
+
+    def segment_in(s):
+        k = f * devices + s
+        return soff_ref[k] + s * tiles * LANES, fst_ref[k], cnt_ref[k]
+
+    move(tile_load(grads_ref), tile_store(vals_ref), tile_load(vals_ref), segment_in, devices, longf_ref[f], slots - 1, vals_ref.shape[0] - 1, lanes16, blank16)
+    ids = lax.broadcasted_iota(jnp.int16, (ROW_SPLIT, 256), 0)
+    sum_ref[...] = jnp.zeros_like(sum_ref)
+
+    def pair(t, _):
+        at = base + 2 * t
+        code = jnp.concatenate([codes_ref[pl.ds(at, 1), :], codes_ref[pl.ds(at + 1, 1), :]], axis=1)
+        low = (code & (ROW_SPLIT - 1)).astype(jnp.int16)
+        used = lane_ids((1, 256), jnp.int32) + t * 256 < total
+        high = jnp.where(used, code >> 9, -1).astype(jnp.int16)
+        onehot = jnp.where(low == ids, jnp.bfloat16(1), jnp.bfloat16(0))
+        vals = jnp.concatenate([vals_ref[2 * t], vals_ref[2 * t + 1]], axis=1)
+        high = jnp.broadcast_to(high, (16, 256))
+        zero = jnp.zeros_like(vals)
+        spread = jnp.concatenate([jnp.where(high == jnp.int16(p), vals, zero) for p in range(parts)], axis=0)
+        sum_ref[...] += lax.dot_general(spread, onehot, (((1,), (1,)), ((), ())), preferred_element_type=jnp.float32)
+        return 0
+
+    lax.fori_loop(0, lax.shift_right_logical(total + 255, 8), pair, 0)
+    for p in range(parts):
+        out_ref[0, :, p * ROW_SPLIT:(p + 1) * ROW_SPLIT] = sum_ref[p * 16:(p + 1) * 16, :]
+
+
+def add_grads(soff, fst, cnt, total, base, longf, codes, grads, tiles, fields, rows_dev):
+    devices = grads.shape[0] // tiles
+    columns = grads.shape[1]
+    fm_tiles = codes.shape[0]
+    kernel = functools.partial(add_kernel, fields, devices, tiles)
+    return pl.pallas_call(
+        kernel,
+        grid_spec=pltpu.PrefetchScalarGridSpec(
+            num_scalar_prefetch=6,
+            grid=(fields,),
+            in_specs=[
+                pl.BlockSpec((fm_tiles, LANES), lambda f, *_: (0, 0)),
+                pl.BlockSpec((devices * tiles, columns, LANES), lambda f, *_: (0, 0, 0)),
+            ],
+            out_specs=pl.BlockSpec((1, columns, rows_dev), lambda f, *_: (f, 0, 0)),
+            scratch_shapes=[
+                pltpu.VMEM((fm_tiles + 2, columns, LANES), jnp.bfloat16),
+                pltpu.VMEM((rows_dev // ROW_SPLIT * columns, ROW_SPLIT), jnp.float32),
+            ],
+        ),
+        out_shape=jax.ShapeDtypeStruct((fields, columns, rows_dev), jnp.float32),
+        compiler_params=params(),
+        name="add_grads",
+    )(soff, fst, cnt, total, base, longf, codes, grads)
 
 
 def local(
@@ -90,10 +478,31 @@
     fields = row_ids.shape[2]
     rows_dev = tables.shape[1]
     columns = tables.shape[2]
-    devices = lax.axis_size(("dp", "wide"))
+    everyone = ("dp", "wide")
+    devices = lax.axis_size(everyone)
     total_events = events * devices
     lookups = events * fields
     capacity = 3 * lookups // (2 * devices)
+    tiles = -(-(capacity + fields) // LANES)
+    fm_tiles = -(-devices * capacity // LANES) + 2 * fields + 2
+
+    ids = jnp.transpose(row_ids, (2, 1, 0))
+    owners, local_rows = ids[:, 0, :], ids[:, 1, :]
+    owned = (owners[:, None, :] == jnp.arange(devices, dtype=jnp.int32)[None, :, None]).astype(jnp.bfloat16)
+    steps = jnp.arange(events, dtype=jnp.int32)
+    upper = (steps[:, None] < steps[None, :]).astype(jnp.bfloat16)
+    before = jnp.einsum("fde,ex->fdx", owned, upper, preferred_element_type=jnp.float32)
+    owned = owned.astype(jnp.float32)
+    cnt = jnp.sum(owned, axis=2).astype(jnp.int32)
+    start = jnp.cumsum(cnt, axis=1) - cnt
+    off = jnp.cumsum(cnt, axis=0) - cnt
+    pos = jnp.sum(owned * (before + start[:, :, None].astype(jnp.float32)), axis=1).astype(jnp.int32)
+    counts = jnp.pad(cnt.T, ((0, 0), (LANES - fields, 0)))
+    long_owner, long_field = jnp.max(cnt, axis=0), jnp.max(cnt, axis=1)
+    start_s, off_s, cnt_s = start.reshape(-1), off.reshape(-1), cnt.reshape(-1)
+    request, inverse = build_request(start_s, off_s, cnt_s, long_owner, pos, local_rows, counts, tiles)
+    asked = lax.all_to_all(request.reshape(devices, tiles, LANES), everyone, split_axis=0, concat_axis=0, tiled=True)
+
     in_b, mid_b, norm_b, gate_b, dense_b = (
         lax.all_gather(in_weight.astype(jnp.bfloat16), "wide", axis=1, tiled=True),
         lax.all_gather(mid_weight.astype(jnp.bfloat16), "wide", axis=1, tiled=True),
@@ -110,33 +519,22 @@
     normed = (dense_in - mean_dense) * inv_dense
     dense_full = dense_b.astype(jnp.float32)
     projected = jnp.dot(normed, dense_full, precision=HIGH)
-    owners = row_ids[:, 0, :].reshape(lookups)
-    local_rows = row_ids[:, 1, :].reshape(lookups)
-    field_of = jnp.arange(lookups, dtype=jnp.int32) % fields
-    codes = field_of * rows_dev + local_rows
-    slots = owners * capacity + owner_positions(owners, devices)
-    request = (
-        jnp.full((devices * capacity,), -1, jnp.int32)
-        .at[slots]
-        .set(codes)
-        .reshape(devices, capacity)
-    )
-    table_count = fields * rows_dev
-    table_pack = packing_for(columns, table_count)
-    wide_table = tables.reshape(table_count // table_pack, table_pack * columns)
-    slot_count = devices * capacity
-    slot_pack = packing_for(columns, slot_count)
-    wanted = lax.all_to_all(request, ("dp", "wide"), split_axis=0, concat_axis=0, tiled=True)
-    valid = wanted >= 0
-    safe_keys = jnp.where(valid, wanted, 0)
-    picked = lane_pick(
-        wide_table[safe_keys // table_pack], safe_keys % table_pack, table_pack, columns
-    )
-    fetched_rows = jnp.where(valid[..., None], picked, 0.0).astype(jnp.bfloat16)
-    returned = lax.all_to_all(fetched_rows, ("dp", "wide"), split_axis=0, concat_axis=0, tiled=True)
-    wide_fetched = returned.reshape(slot_count // slot_pack, slot_pack * columns)
-    looked = lane_pick(wide_fetched[slots // slot_pack], slots % slot_pack, slot_pack, columns)
-    looked = looked.astype(jnp.bfloat16).reshape(events, fields * columns)
+
+    got_cnt = asked[:, tiles - 1, LANES - fields:].T
+    soff = jnp.cumsum(got_cnt, axis=0) - got_cnt
+    fst = jnp.cumsum(got_cnt, axis=1) - got_cnt
+    total = jnp.sum(got_cnt, axis=1)
+    pairs = (total + 2 * LANES - 1) // (2 * LANES) * 2
+    base = jnp.cumsum(pairs) - pairs
+    long_source, long_in = jnp.max(got_cnt, axis=0), jnp.max(got_cnt, axis=1)
+    soff_s, fst_s, got_s = soff.reshape(-1), fst.reshape(-1), got_cnt.reshape(-1)
+    tables_t = jnp.transpose(tables, (0, 2, 1))
+    fetched, codes = fetch_rows(
+        soff_s, fst_s, got_s, total, base, long_in, long_source, asked.reshape(devices * tiles, LANES), tables_t, tiles, fm_tiles
+    )
+    returned = lax.all_to_all(fetched.reshape(devices, tiles, columns, LANES), everyone, split_axis=0, concat_axis=0, tiled=True)
+    looked = unsort_rows(start_s, off_s, cnt_s, long_field, pos, returned.reshape(devices * tiles, columns, LANES), tiles)
+    looked = looked.reshape(fields * columns, events).T
     features = jnp.concatenate([looked, projected.astype(jnp.bfloat16)], axis=1)
     logits = jnp.dot(features, gate_b, preferred_element_type=jnp.float32)
     gate_a = jax.nn.softmax(logits[:, 0:4], axis=-1)
@@ -185,27 +583,13 @@
     d_projected = d_features[:, fields * columns :]
     dense_grad_w = jnp.einsum("bi,bo->io", normed, d_projected, precision=HIGH)
     d_normed = jnp.einsum("bo,io->bi", d_projected, dense_full, precision=HIGH)
-    spread_out = lane_spread(d_looked.reshape(lookups, columns), slots % slot_pack, slot_pack)
-    outgoing = (
-        jnp.zeros((slot_count // slot_pack, slot_pack * columns), jnp.float32)
-        .at[slots // slot_pack]
-        .add(spread_out)
-    )
-    arrived = lax.all_to_all(
-        outgoing.reshape(devices, capacity, columns),
-        ("dp", "wide"),
-        split_axis=0,
-        concat_axis=0,
-        tiled=True,
-    )
-    valid_in = wanted >= 0
-    target_keys = jnp.where(valid_in, wanted, 0).reshape(-1)
-    target_rows = jnp.where(valid_in, wanted // table_pack, table_count // table_pack).reshape(-1)
-    spread_in = lane_spread(arrived.reshape(-1, columns), target_keys % table_pack, table_pack)
-    table_grad = jax.ops.segment_sum(
-        spread_in, target_rows, num_segments=table_count // table_pack + 1
-    )
-    table_grad = table_grad[: table_count // table_pack].reshape(fields, rows_dev, columns)
+    d_looked = d_looked.astype(jnp.bfloat16).T.reshape(fields, columns, events)
+    outgoing = sort_grads(start_s, off_s, cnt_s, long_owner, inverse, d_looked, tiles)
+    arrived = lax.all_to_all(outgoing.reshape(devices, tiles, columns, LANES), everyone, split_axis=0, concat_axis=0, tiled=True)
+    table_grad = add_grads(
+        soff_s, fst_s, got_s, total, base, long_in, codes, arrived.reshape(devices * tiles, columns, LANES), tiles, fields, rows_dev
+    )
+    table_grad = jnp.transpose(table_grad, (0, 2, 1))
     back_sum = jnp.sum(d_normed, axis=0)
     back_cross = jnp.sum(d_normed * normed, axis=0)
     shards = (

time: 1540 us -> 564 us (0.37)
  local copies, waits for them, and re-layouts: 760 us -> 37.6 us
  other arithmetic: 449 us -> 34.8 us
  Pallas kernels: 0 us -> 210 us
  waiting for transfers between devices: 29.7 us -> 0.16 us
    scatter-add x2 -> x0, other arithmetic: 381 us -> none  [the longest x1 239 us: local(): jax.ops.segment_sum(spread_in, target_rows, num_segments=table_count // t...]
    gather x2 -> x0, local copies, waits for them, and re-layouts: 231 us -> none  [the longest x1 138 us: local(): wide_table[safe_keys // table_pack]]
    pallas_call x0 -> x5, Pallas kernels: none -> 210 us  [the longest x1 69 us: fetch_rows(): pl.pallas_call(kernel, grid_spec=pltpu.PrefetchScalarGridSpec(num_scalar_...]
    reshape x5 -> x6, local copies, waits for them, and re-layouts: 152 us -> 0.78 us  [the longest x1 0.52 us: local(): looked = looked.reshape(fields * columns, events).T]
    scatter x1 -> x0, local copies, waits for them, and re-layouts: 97.7 us -> none  [local(): request = jnp.full((devices * capacity,), -1, jnp.int32).at[slots].set(co...]
    unnamed x155 -> x96, local copies, waits for them, and re-layouts: 116 us -> 19 us
    convert_element_type x7 -> x4, local copies, waits for them, and re-layouts: 63.5 us -> 0.32 us  [the longest x2 0.16 us: local(): cnt = jnp.sum(owned, axis=2).astype(jnp.int32)]
    select_n x3 -> x0, local copies, waits for them, and re-layouts: 35.8 us -> none  [the longest x2 35.7 us: lane_spread(): spread = jnp.where(chosen[..., None], values[..., None, :], 0.0)]
  transfers between devices with their start and end apart: 9 -> 8, of which waited for: 1 -> 0; matrix products, arithmetic and copies ran while one was open for 79% -> 14% of each run, Pallas kernels for 0% -> 20%
where the time goes in v1:
time: 564 us; the launch traced here: 557 us
  Pallas kernels  210 us (37%)
  blocking collectives  180 us (32%)
  matrix products  72.3 us (13%)
  local copies, waits for them, and re-layouts  37.6 us (7%)
  other arithmetic  34.8 us (6%)
  between operations  15.9 us (3%)
  starting transfers between devices  6.13 us (1%)
    pallas_call x1, Pallas kernels, fetch_rows(): pl.pallas_call(kernel, grid_spec=pltpu.PrefetchScalarGridSpec(num_scalar_...  69 us
    pallas_call x1, Pallas kernels, add_grads(): pl.pallas_call(kernel, grid_spec=pltpu.PrefetchScalarGridSpec(num_scalar_...  63.1 us
    psum x1, blocking collectives, local(): total_sum, total_cross = lax.psum((back_sum, back_cross), ('dp', 'wide'))  48.5 us
    psum x1, blocking collectives, local(): lax.psum((jnp.sum(dense_in, axis=0), jnp.sum(dense_in * dense_in, axis=0)...  48.2 us
    pallas_call x1, Pallas kernels, build_request(): pl.pallas_call(kernel, grid_spec=pltpu.PrefetchScalarGridSpec(num_scalar_...  28.3 us
    pallas_call x1, Pallas kernels, sort_grads(): pl.pallas_call(kernel, grid_spec=pltpu.PrefetchScalarGridSpec(num_scalar_...  25.6 us
    pallas_call x1, Pallas kernels, unsort_rows(): pl.pallas_call(kernel, grid_spec=pltpu.PrefetchScalarGridSpec(num_scalar_...  23.7 us
    unnamed x96, local copies, waits for them, and re-layouts  19 us
  transfers between devices with their start and end apart: 8, of which 0 were waited for; matrix products, arithmetic and copies ran while one was open for 14% of the time, Pallas kernels for 20%

profile of v1, /device:TPU:1, one launch (start us, length us, event | category | flops | bytes accessed | tf_op | source)
XLA Modules:
  0.0 556.9 jit_solution(9777747418705595556)
XLA Ops:
  12.3 28.3 %build_request.1 = (s32[320,128]{1,0:T(8,128)S(1)}, s32[26,1,1024]{2,1,0:T(1,128)S(1)}) custom-call(s32[832]{0:T(1024)S(1)} %get-tuple-element.162.start_ref, s32[832]{0:T(1024)S(1)} %get-tuple-element.161.off_ref, s32[832]{0:T(1024)S(1)} %convert_element_type.88.cnt_ref, s32[32]{0:T(128)S(1)} %get-tuple-element.113.longest_ref, ...), custom_call_target="tpu_custom_call" | custom-call | tf_op jit(solution)/shard_map/build_request/pallas_call | solution.py:191
  40.7 17.2 %all_to_all.15 = s32[32,10,128]{2,1,0:T(8,128)S(1)} all-to-all(s32[32,10,128]{2,1,0:T(8,128)S(1)} %reshape.211), channel_id=1, replica_groups=mesh['dp'=4,'wide'=8] {'dp','wide'}, dimensions={0} | all-to-all | bytes 327680 | tf_op jit(solution)/shard_map/all_to_all | solution.py:504
  59.5 69.0 %fetch_rows.1 = (bf16[320,16,128]{2,1,0:T(8,128)(2,1)}, s32[366,128]{1,0:T(8,128)S(1)}) custom-call(s32[832]{0:T(1024)S(1)} %reshape.212.soff_ref, s32[832]{0:T(1024)S(1)} %reshape.213.fst_ref, s32[832]{0:T(1024)S(1)} %reshape.214.cnt_ref, s32[26]{0:T(128)S(1)} %get-tuple-element.103.total_ref, s32[26]{0:T(128)S(1)} %multiply_subtract_fusion.3.base_ref, ...), custom_call_target="tpu_custom_call" | custom-call | tf_op jit(solution)/shard_map/fetch_rows/pallas_call | solution.py:273
  131.9 48.2 %all-reduce.4 = (f32[13]{0:T(128)S(1)}, f32[13]{0:T(128)S(1)}) all-reduce(f32[13]{0:T(128)S(1)} %get-tuple-element.112, f32[13]{0:T(128)S(1)} %get-tuple-element.111), channel_id=1, replica_groups=mesh['dp'=4,'wide'=8] {'dp','wide'}, use_global_device_ids=true, to_apply=%region_15.16 | all-reduce | flops 26 | bytes 208 | tf_op jit(solution)/shard_map/psum | solution.py:513
  180.3 11.1 %all-gather = bf16[8,12,13]{2,1,0:T(8,128)(2,1)S(1)} all-gather(bf16[1,12,13]{2,1,0:T(8,128)(2,1)S(1)} %bitcast.169), channel_id=1, replica_groups=mesh['dp'=4,'wide'=8] {'wide'}, dimensions={0}, use_global_device_ids=true | all-gather | bytes 2808 | tf_op jit(solution)/shard_map/all_gather | solution.py:511
  191.5 8.0 %all-gather.1 = bf16[8,64,14]{1,2,0:T(8,128)(2,1)S(1)} all-gather(bf16[1,64,14]{1,2,0:T(8,128)(2,1)S(1)} %convert_bitcast_fusion), channel_id=1, replica_groups=mesh['dp'=4,'wide'=8] {'wide'}, dimensions={0}, use_global_device_ids=true | all-gather | bytes 16128 | tf_op jit(solution)/shard_map/all_gather | solution.py:510
  199.7 9.3 %all_gather.19 = bf16[6,2,256]{0,1,2:T(2,128)(2,1)S(1)} all-gather(bf16[6,2,32]{0,1,2:T(2,128)(2,1)S(1)} %copy.175), channel_id=1, replica_groups=mesh['dp'=4,'wide'=8] {'wide'}, dimensions={2}, use_global_device_ids=true | all-gather | bytes 6912 | tf_op jit(solution)/shard_map/all_gather | solution.py:509
  214.8 11.0 %all_gather.18 = bf16[6,256,256]{2,1,0:T(8,128)(2,1)} all-gather(bf16[6,32,256]{2,1,0:T(8,128)(2,1)S(1)} %convert_element_type.98), channel_id=1, replica_groups=mesh['dp'=4,'wide'=8] {'wide'}, dimensions={1}, use_global_device_ids=true | all-gather | bytes 884736 | tf_op jit(solution)/shard_map/all_gather | solution.py:508
  225.8 23.7 %unsort_rows.1 = bf16[26,16,1024]{2,1,0:T(8,128)(2,1)S(1)} custom-call(s32[832]{0:T(1024)S(1)} %get-tuple-element.162.start_ref, s32[832]{0:T(1024)S(1)} %get-tuple-element.161.off_ref, s32[832]{0:T(1024)S(1)} %convert_element_type.88.cnt_ref, s32[26]{0:T(128)S(1)} %get-tuple-element.114.longest_ref, s32[26,1,1024]{2,1,0:T(1,128)S(1)} %convert_element_type.91.pos_ref, ...), custom_call_target="tpu_custom_call" | custom-call | tf_op jit(solution)/shard_map/unsort_rows/pallas_call | solution.py:323
  255.0 4.6 fusion.65
  268.4 9.9 %fusion = f32[1024,6,3]{1,2,0:T(4,128)} fusion(bf16[1024,3,256]{2,1,0:T(4,128)(2,1)S(1)} %copy-done.3, f32[6,1024,256]{2,1,0:T(8,128)S(1)} %multiply_add_fusion), kind=kOutput, calls=%fused_computation.4 | convolution fusion | flops 56623104 | bytes 7938048 | tf_op jit(solution)/shard_map/bgh,ebh->bge/dot_general | solution.py:558
  282.3 6.4 %fusion.73 = f32[1024,6,256]{2,1,0:T(8,128)S(1)} fusion(f32[1024,3,6]{2,1,0:T(4,128)} %copy.177, bf16[1024,3,256]{2,1,0:T(4,128)(2,1)S(1)} %copy-done.3), kind=kOutput, calls=%fused_computation.160 | convolution fusion | flops 56623104 | bytes 7938048 | tf_op jit(solution)/shard_map/bge,bgh->ebh/dot_general | solution.py:557
  288.8 9.4 %fusion.18 = (f32[6,256]{1,0:T(8,128)S(1)}, f32[6,1024]{1,0:T(8,128)S(1)}, f32[6,1024]{1,0:T(8,128)S(1)}, f32[6,256]{1,0:T(8,128)S(1)}) fusion(f32[6,1024]{1,0:T(8,128)S(1)} %add_rsqrt_fusion, f32[6,1024]{1,0:T(8,128)S(1)} %broadcast_multiply_fusion.2, f32[1024,6,256]{2,1,0:T(8,128)S(1)} %fusion.73, f32[6,1024,256]{2,1,0:T(8,128)} %copy-done, ...), kind=kLoop, calls=%fused_computation.25 | loop fusion | flops 26723328 | bytes 12699648 | tf_op jit(solution)/shard_map/reduce_sum | solution.py:565
  300.7 10.7 %fusion.17 = bf16[6,1024,256]{2,1,0:T(8,128)(2,1)S(1)} fusion(f32[6,1024,256]{2,1,0:T(8,128)} %copy-done, f32[6,1024]{1,0:T(8,128)S(1)} %get-tuple-element.170, f32[6,1024]{1,0:T(8,128)S(1)} %get-tuple-element.171, f32[6,256]{1,0:T(8,128)S(1)} %get-tuple-element.153, f32[6,1024]{1,0:T(8,128)S(1)} %add_rsqrt_fusion, ...), kind=kLoop, calls=%fused_computation.21 | loop fusion | flops 44040192 | bytes 15833088 | tf_op jit(solution)/shard_map/convert_element_type | solution.py:572
  313.1 6.6 %fusion.61 = f32[6,256,256]{2,1,0:T(8,128)} fusion(bf16[6,1024,256]{2,1,0:T(8,128)(2,1)S(1)} %fusion.17, f32[1024,6,256]{2,0,1:T(8,128)} %copy-done.5), kind=kOutput, calls=%fused_computation.152 | convolution fusion | flops 819462144 | bytes 11010048 | tf_op jit(solution)/shard_map/ebh,ebk->ehk/dot_general | solution.py:573
  319.8 8.0 %fusion.10 = bf16[6,1024,256]{2,1,0:T(8,128)(2,1)S(1)} fusion(f32[1024,6,256]{2,0,1:T(8,128)} %copy-done.5, bf16[6,1024,256]{2,1,0:T(8,128)(2,1)} %copy-done.8, bf16[6,256,256]{2,1,0:T(8,128)(2,1)S(1)} %copy-done.15), kind=kOutput, calls=%fused_computation.14 | convolution fusion | flops 836763648 | bytes 13369344 | tf_op jit(solution)/shard_map/ebk,ehk->ebh/dot_general | solution.py:574
  333.0 5.2 copy.189
  338.2 3.7 fusion.74
  343.9 25.6 %sort_grads.1 = bf16[320,16,128]{2,1,0:T(8,128)(2,1)} custom-call(s32[832]{0:T(1024)S(1)} %get-tuple-element.162.start_ref, s32[832]{0:T(1024)S(1)} %get-tuple-element.161.off_ref, s32[832]{0:T(1024)S(1)} %convert_element_type.88.cnt_ref, s32[32]{0:T(128)S(1)} %get-tuple-element.113.longest_ref, s32[26,1,1024]{2,1,0:T(1,128)S(1)} %get-tuple-element.25.inv_ref, ...), custom_call_target="tpu_custom_call" | custom-call | tf_op jit(solution)/shard_map/sort_grads/pallas_call | solution.py:375
  375.7 48.5 %all-reduce.3 = (f32[13]{0:T(128)S(1)}, f32[13]{0:T(128)S(1)}) all-reduce(f32[13]{0:T(128)S(1)} %get-tuple-element.106, f32[13]{0:T(128)S(1)} %get-tuple-element.105), channel_id=1, replica_groups=mesh['dp'=4,'wide'=8] {'dp','wide'}, use_global_device_ids=true, to_apply=%region_32.33 | all-reduce | flops 26 | bytes 208 | tf_op jit(solution)/shard_map/psum | solution.py:603
  424.2 17.6 %fusion.28 = bf16[1024,3,256]{2,1,0:T(4,128)(2,1)} fusion(f32[1024,3,6]{2,1,0:T(4,128)} %copy.177, f32[6,1024,256]{2,1,0:T(8,128)} %copy-done.1), kind=kOutput, calls=%fused_computation.46 | convolution fusion | flops 57409536 | bytes 7938048 | tf_op jit(solution)/shard_map/bge,ebh->bgh/dot_general | solution.py:554
  447.8 12.9 %all-reduce.2 = f32[13,96]{1,0:T(8,128)S(1)} all-reduce(f32[13,96]{1,0:T(8,128)S(1)} %fusion.39), channel_id=6, replica_groups=mesh['dp'=4,'wide'=8] {'wide'}, use_global_device_ids=true, to_apply=%region_43.44.clone | all-reduce | flops 1248 | bytes 9984
  463.2 14.1 %all-reduce.5 = (f32[6,2,32]{2,0,1:T(8,128)S(1)}, f32[64,14]{0,1:T(8,128)S(1)}, f32[13,12]{1,0:T(8,128)S(1)}) all-reduce(f32[6,2,32]{2,0,1:T(8,128)S(1)} %copy.209, f32[64,14]{0,1:T(8,128)S(1)} %copy.211, f32[13,12]{1,0:T(8,128)S(1)} %constant_dynamic-slice_fusion), channel_id=1, replica_groups=mesh['dp'=4,'wide'=8] {'dp'}, use_global_device_ids=true, to_apply=%region_40.41 | all-reduce | flops 1436 | bytes 11488 | tf_op jit(solution)/shard_map/psum | solution.py:602
  480.5 63.1 %add_grads.1 = f32[26,16,8192]{2,1,0:T(8,128)} custom-call(s32[832]{0:T(1024)S(1)} %reshape.212.soff_ref, s32[832]{0:T(1024)S(1)} %reshape.213.fst_ref, s32[832]{0:T(1024)S(1)} %reshape.214.cnt_ref, s32[26]{0:T(128)S(1)} %get-tuple-element.103.total_ref, s32[26]{0:T(128)S(1)} %multiply_subtract_fusion.3.base_ref, s32[26]{0:T(128)S(1)} %get-tuple-element.104.longf_ref, ...), custom_call_target="tpu_custom_call" | custom-call | tf_op jit(solution)/shard_map/add_grads/pallas_call | solution.py:435
  (204 shorter events, 68.9 us)
Async XLA Ops:
  12.1 118.8 %copy-start.11 = (f32[6,64,256]{2,1,0:T(8,128)S(1)}, f32[6,64,256]{2,1,0:T(8,128)}, u32[]{:S(2)}) copy-start(f32[6,64,256]{2,1,0:T(8,128)} %param.23) | copy-start | bytes 1179652
  12.2 119.6 %copy-start.9 = (f32[1024,13]{0,1:T(8,128)S(1)}, f32[1024,13]{0,1:T(8,128)}, u32[]{:S(2)}) copy-start(f32[1024,13]{0,1:T(8,128)} %param.20) | copy-start | bytes 159748
  12.3 167.9 %copy-start.26 = (f32[6,2,32]{2,1,0:T(2,128)S(1)}, f32[6,2,32]{2,1,0:T(2,128)}, u32[]{:S(2)}) copy-start(f32[6,2,32]{2,1,0:T(2,128)} %param.29) | copy-start | bytes 4612
  12.3 167.9 %copy-start.24 = (f32[13,12]{1,0:T(8,128)S(1)}, f32[13,12]{1,0:T(8,128)}, u32[]{:S(2)}) copy-start(f32[13,12]{1,0:T(8,128)} %param.35) | copy-start | bytes 1876
  12.3 179.2 %copy-start.22 = (f32[64,14]{0,1:T(8,128)S(1)}, f32[64,14]{0,1:T(8,128)}, u32[]{:S(2)}) copy-start(f32[64,14]{0,1:T(8,128)} %param.32) | copy-start | bytes 10756
  40.7 159.0 %copy-start.16 = (f32[6,32,256]{2,1,0:T(8,128)S(1)}, f32[6,32,256]{2,1,0:T(8,128)}, u32[]{:S(2)}) copy-start(f32[6,32,256]{2,1,0:T(8,128)} %param.26) | copy-start | bytes 589828
  128.5 97.3 %all-to-all-start.1 = ((bf16[32,10,16,128]{3,2,1,0:T(8,128)(2,1)}), bf16[32,10,16,128]{3,2,1,0:T(8,128)(2,1)S(1)}, u32[]{:S(2)}, u32[]{:S(2)}) async-start(bf16[32,10,16,128]{3,2,1,0:T(8,128)(2,1)} %bitcast.8), calls=%async_computation.1 | async-start | bytes 2621440 | tf_op jit(solution)/shard_map/all_to_all | solution.py:535
  130.9 120.9 %all-gather.4.cloned.1.call-start = ((), (), s32[]{:S(2)}) async-start(), calls=%async_computation.7 | async-start | bytes 1769472 | tf_op jit(solution)/shard_map/all_gather | solution.py:507
  131.7 329.8 %reduce-scatter.14.cloned.1.call-start = ((), (), s32[]{:S(2)}) async-start(), calls=%async_computation.10 | async-start | bytes 147456
  299.2 163.1 %reduce-scatter.16.cloned.1.call-start = ((), (), s32[]{:S(2)}) async-start(), calls=%async_computation.11 | async-start | bytes 294912
  300.6 176.7 %reduce-scatter.12.cloned.1.call-start = ((), (), s32[]{:S(2)}) async-start(), calls=%async_computation.9 | async-start | bytes 1769472 | tf_op jit(solution)/shard_map/reduce_scatter | solution.py:597
  319.8 157.6 %reduce-scatter.10.cloned.1.call-start = ((), (), s32[]{:S(2)}) async-start(), calls=%async_computation.8 | async-start | bytes 4718592 | tf_op jit(solution)/shard_map/reduce_scatter | solution.py:596
  369.5 110.9 %all-to-all-start.2 = ((bf16[32,10,16,128]{3,2,1,0:T(8,128)(2,1)}), bf16[32,10,16,128]{3,2,1,0:T(8,128)(2,1)S(1)}, u32[]{:S(2)}, u32[]{:S(2)}) async-start(bf16[32,10,16,128]{3,2,1,0:T(8,128)(2,1)} %bitcast.33), calls=%async_computation.2 | async-start | bytes 2621440 | tf_op jit(solution)/shard_map/all_to_all | solution.py:588
  373.0 170.6 %all-reduce.9.cloned.1.call-start = ((), (), s32[]{:S(2)}) async-start(), calls=%async_computation.12 | async-start | bytes 1441792 | tf_op jit(solution)/shard_map/psum | solution.py:602
  441.7 37.5 %copy-start.23 = (f32[64,14]{0,1:T(8,128)S(1)}, f32[64,14]{0,1:T(8,128)}, u32[]{:S(2)}) copy-start(f32[64,14]{0,1:T(8,128)} %param.32) | copy-start | bytes 10756
  441.7 38.1 %copy-start.25 = (f32[13,12]{1,0:T(8,128)S(1)}, f32[13,12]{1,0:T(8,128)}, u32[]{:S(2)}) copy-start(f32[13,12]{1,0:T(8,128)} %param.35) | copy-start | bytes 1876
  441.8 38.1 %copy-start.32 = (f32[13,12]{1,0:T(8,128)S(1)}, f32[13,12]{1,0:T(8,128)}, u32[]{:S(2)}) copy-start(f32[13,12]{1,0:T(8,128)} %param.37) | copy-start | bytes 1876
  441.8 38.1 %copy-start.33 = (f32[13,12]{1,0:T(8,128)S(1)}, f32[13,12]{1,0:T(8,128)}, u32[]{:S(2)}) copy-start(f32[13,12]{1,0:T(8,128)} %param.36) | copy-start | bytes 1876
  480.5 63.2 %copy-start.12 = (f32[6,64,256]{2,1,0:T(8,128)S(1)}, f32[6,64,256]{2,1,0:T(8,128)}, u32[]{:S(2)}) copy-start(f32[6,64,256]{2,1,0:T(8,128)} %param.23) | copy-start | bytes 1179652
  480.5 63.2 %copy-start.18 = (f32[6,64,256]{2,1,0:T(8,128)S(1)}, f32[6,64,256]{2,1,0:T(8,128)}, u32[]{:S(2)}) copy-start(f32[6,64,256]{2,1,0:T(8,128)} %param.25) | copy-start | bytes 1179652
  480.5 63.2 %copy-start.19 = (f32[6,64,256]{2,1,0:T(8,128)S(1)}, f32[6,64,256]{2,1,0:T(8,128)}, u32[]{:S(2)}) copy-start(f32[6,64,256]{2,1,0:T(8,128)} %param.24) | copy-start | bytes 1179652
  480.5 67.6 %copy-start.17 = (f32[6,32,256]{2,1,0:T(8,128)S(1)}, f32[6,32,256]{2,1,0:T(8,128)}, u32[]{:S(2)}) copy-start(f32[6,32,256]{2,1,0:T(8,128)} %param.26) | copy-start | bytes 589828
  480.5 67.6 %copy-start.20 = (f32[6,32,256]{2,1,0:T(8,128)S(1)}, f32[6,32,256]{2,1,0:T(8,128)}, u32[]{:S(2)}) copy-start(f32[6,32,256]{2,1,0:T(8,128)} %param.28) | copy-start | bytes 589828
  480.5 67.6 %copy-start.21 = (f32[6,32,256]{2,1,0:T(8,128)S(1)}, f32[6,32,256]{2,1,0:T(8,128)}, u32[]{:S(2)}) copy-start(f32[6,32,256]{2,1,0:T(8,128)} %param.27) | copy-start | bytes 589828
  (22 other events, 350.3 us)
Sparse Core Ops, SparseCore 0:
  134.2 28.7 all-gather.3
  299.4 31.3 reduce-scatter.13
  334.7 33.6 reduce-scatter.15
  371.5 40.3 reduce-scatter.11
  415.7 51.4 reduce-scatter.9
  477.5 43.7 all-reduce.8
